TPU v7x, 32 devices: a whole 2x2x4 slice. The times are simulated.
32 devices in a mesh: wide: 16 (over z, x, core), heads: 2 (over y).
Axes of the slice: x: 2, y: 2, z: 4, core: 2. Of those that a mesh axis runs over, the one named last changes fastest.
Arguments:
- inputs: bfloat16 [32768, 1280], P('wide'), may hold values from -6 to 6
- segment_ids: int32 [32768], P('wide'), may hold values from 0 to 4095, never falling along the last dimension, each value on 1 to 16 neighbouring positions
- cotangent: bfloat16 [32768, 1280], P('wide'), may hold values from -6 to 6
- w_query: bfloat16 [1280, 1280], P('wide', 'heads'), may hold values from -0.15625 to 0.15625
- w_key: bfloat16 [1280, 1280], P('wide', 'heads'), may hold values from -0.15625 to 0.15625
- w_value: bfloat16 [1280, 1280], P('wide', 'heads'), may hold values from -0.15625 to 0.15625
- w_out: bfloat16 [1280, 1280], P('heads', 'wide'), may hold values from -0.3125 to 0.3125
- w_up: bfloat16 [1280, 1280], P('wide', 'heads'), may hold values from -0.15625 to 0.15625
- w_down: bfloat16 [1280, 1280], P('heads', 'wide'), may hold values from -0.25 to 0.25
- b_query: float32 [1280], replicated, may hold values from -3 to 3
- b_value: float32 [1280], replicated, may hold values from -3 to 3
- b_out: float32 [1280], replicated, may hold values from -3 to 3
- b_up: float32 [1280], replicated, may hold values from -3 to 3
- b_down: float32 [1280], replicated, may hold values from -3 to 3
- dim_scale: float32 [80], replicated, may hold values from -1 to 1.5
- gain_attn: float32 [1280], replicated, may hold values from 0.5 to 1.5
- gain_mlp: float32 [1280], replicated, may hold values from 0.5 to 1.5
Outputs:
- output: bfloat16 [32768, 1280], P(('wide', 'heads'))
- input_grad: float32 [32768, 1280], P(('wide', 'heads'))
- grad_w_query: float32 [1280, 1280], P('wide', 'heads')
- grad_w_key: float32 [1280, 1280], P('wide', 'heads')
- grad_w_value: float32 [1280, 1280], P('wide', 'heads')
- grad_w_out: float32 [1280, 1280], P('heads', 'wide')
- grad_w_up: float32 [1280, 1280], P('wide', 'heads')
- grad_w_down: float32 [1280, 1280], P('heads', 'wide')
- grad_b_query: float32 [1280], replicated
- grad_b_value: float32 [1280], replicated
- grad_b_out: float32 [1280], replicated
- grad_b_up: float32 [1280], replicated
- grad_b_down: float32 [1280], replicated
- grad_dim_scale: float32 [80], replicated
- grad_gain_attn: float32 [1280], replicated
- grad_gain_mlp: float32 [1280], replicated
Inputs may be any that keep to these rules, and one draw needn't show every extreme that they name: `segment_ids`: segment numbers never fall along the tokens; a segment has 1 to 16 tokens.
All inputs are finite; a program needn't handle non-finite values.
Results may differ from a plain program's by a relative error of at most 0.015.
Values may be sent and summed in bfloat16 or wider, within the bound.
A program may use at most 192 MiB of HBM per device.

v0:
```python
import math
import jax
import jax.numpy as jnp
from jax import lax
from jax.sharding import PartitionSpec as P

DH = 80
PATCHES = 16
eps = 1e-06
query_base = 1.442695041


def dot_plain(left, right):
    return jnp.dot(left, right, preferred_element_type=jnp.float32)


def dot_left(left, right):
    return lax.dot_general(
        left, right, (((0,), (0,)), ((), ())), preferred_element_type=jnp.float32
    )


def dot_right(left, right):
    return lax.dot_general(
        left, right, (((1,), (1,)), ((), ())), preferred_element_type=jnp.float32
    )


def inverse_rms(values):
    return lax.rsqrt(jnp.mean(values * values, axis=-1, keepdims=True) + eps)


def norm_back(values, gain_vec, grad_in):
    factor = inverse_rms(values)
    inner = jnp.mean(grad_in * gain_vec * values, axis=-1, keepdims=True)
    grad_out = factor * gain_vec * grad_in - values * factor * factor * factor * inner
    return (grad_out, jnp.sum(grad_in * values * factor, axis=0))


def tile_mask(seg_tiles, tile_len):
    position = jnp.arange(tile_len)
    same_row = position[:, None] // PATCHES == position[None, :] // PATCHES
    causal = position[:, None] >= position[None, :]
    same_seg = seg_tiles[:, :, None] == seg_tiles[:, None, :]
    return (same_seg & (same_row & causal)[None])[:, None]


def masked_scores(query_tiles, key_tiles, allowed):
    scores = jnp.einsum(
        "bqhe,bkhe->bhqk", query_tiles, key_tiles, preferred_element_type=jnp.float32
    )
    return jnp.where(allowed, scores, -1e30)


def place_part(vector, length, offset):
    return lax.dynamic_update_slice_in_dim(jnp.zeros((length,), jnp.float32), vector, offset, 0)


def shards(
    inputs,
    segment_ids,
    cotangent,
    w_query,
    w_key,
    w_value,
    w_out,
    w_up,
    w_down,
    b_query,
    b_value,
    b_out,
    b_up,
    b_down,
    dim_scale,
    gain_attn,
    gain_mlp,
):
    tok_rows = inputs.shape[0]
    head_groups = lax.axis_size("heads")
    head_index = lax.axis_index("heads")
    half_rows = tok_rows // head_groups
    local_hd = w_query.shape[1]
    local_ff = w_up.shape[1]
    local_heads = local_hd // DH
    tile_len = min(128, tok_rows)
    tile_count = tok_rows // tile_len
    row_start = head_index * half_rows
    input_full = inputs.astype(jnp.float32)
    input_half = lax.dynamic_slice_in_dim(input_full, row_start, half_rows, 0)
    cot_half = lax.dynamic_slice_in_dim(cotangent, row_start, half_rows, 0)
    grad_half = cot_half.astype(jnp.float32)
    bias_query = lax.dynamic_slice_in_dim(b_query, head_index * local_hd, local_hd, 0)
    bias_value = lax.dynamic_slice_in_dim(b_value, head_index * local_hd, local_hd, 0)
    bias_up = lax.dynamic_slice_in_dim(b_up, head_index * local_ff, local_ff, 0)
    scale_const = query_base / math.sqrt(DH)
    query_scale = scale_const * jax.nn.softplus(dim_scale)
    tile_shape = (tile_count, tile_len, local_heads, DH)
    query_full, key_full, value_full, out_full = (
        lax.all_gather(w_query, "wide", axis=0, tiled=True),
        lax.all_gather(w_key, "wide", axis=0, tiled=True),
        lax.all_gather(w_value, "wide", axis=0, tiled=True),
        lax.all_gather(w_out, "wide", axis=1, tiled=True),
    )
    normed_one = (input_full * inverse_rms(input_full) * gain_attn).astype(jnp.bfloat16)
    query_proj = dot_plain(normed_one, query_full) + bias_query
    query_tiles = (query_proj.reshape(tile_shape) * query_scale).astype(jnp.bfloat16)
    key_tiles = dot_plain(normed_one, key_full).astype(jnp.bfloat16).reshape(tile_shape)
    value_tiles = (
        (dot_plain(normed_one, value_full) + bias_value).astype(jnp.bfloat16).reshape(tile_shape)
    )
    allowed = tile_mask(segment_ids.reshape(tile_count, tile_len), tile_len)
    scores = masked_scores(query_tiles, key_tiles, allowed)
    row_max = jnp.max(scores, axis=-1, keepdims=True)
    exp_scores = jnp.exp(scores - row_max)
    row_total = jnp.sum(exp_scores, axis=-1, keepdims=True)
    attn_probs = exp_scores / row_total
    log_total = row_max + jnp.log(row_total)
    attended = jnp.einsum(
        "bhqk,bkhe->bqhe",
        attn_probs.astype(jnp.bfloat16),
        value_tiles,
        preferred_element_type=jnp.float32,
    )
    attended = attended.reshape(tok_rows, local_hd).astype(jnp.bfloat16)
    up_full, down_full = (
        lax.all_gather(w_up, "wide", axis=0, tiled=True),
        lax.all_gather(w_down, "wide", axis=1, tiled=True),
    )
    attn_half = lax.psum_scatter(
        dot_plain(attended, out_full), "heads", scatter_dimension=0, tiled=True
    )
    residual = input_half + attn_half + b_out
    normed_half = (residual * inverse_rms(residual) * gain_mlp).astype(jnp.bfloat16)
    normed_two = lax.all_gather(normed_half, "heads", axis=0, tiled=True)
    up_proj = dot_plain(normed_two, up_full) + bias_up
    activated = jax.nn.gelu(up_proj).astype(jnp.bfloat16)
    mlp_half = lax.psum_scatter(
        dot_plain(activated, down_full).astype(jnp.bfloat16),
        "heads",
        scatter_dimension=0,
        tiled=True,
    ).astype(jnp.float32)
    output = (residual + mlp_half + b_down).astype(jnp.bfloat16)
    up_full, down_full = (
        lax.all_gather(w_up, "wide", axis=0, tiled=True),
        lax.all_gather(w_down, "wide", axis=1, tiled=True),
    )
    grad_down = dot_left(activated, cotangent)
    grad_act = dot_right(cotangent, down_full)
    unused_value, gelu_pull = jax.vjp(jax.nn.gelu, up_proj)
    grad_up_proj = gelu_pull(grad_act)[0].astype(jnp.bfloat16)
    grad_up = dot_left(normed_two, grad_up_proj)
    bias_up_term = place_part(
        jnp.sum(grad_up_proj.astype(jnp.float32), axis=0), b_up.shape[0], head_index * local_ff
    )
    grad_norm_two = lax.psum_scatter(
        dot_right(grad_up_proj, up_full).astype(jnp.bfloat16),
        "heads",
        scatter_dimension=0,
        tiled=True,
    ).astype(jnp.float32)
    back_two, grad_gain_two = norm_back(residual, gain_mlp, grad_norm_two)
    grad_resid = grad_half + back_two
    branch_half = grad_resid.astype(jnp.bfloat16)
    query_full, key_full, value_full, out_full = (
        lax.all_gather(w_query, "wide", axis=0, tiled=True),
        lax.all_gather(w_key, "wide", axis=0, tiled=True),
        lax.all_gather(w_value, "wide", axis=0, tiled=True),
        lax.all_gather(w_out, "wide", axis=1, tiled=True),
    )
    grad_branch = lax.all_gather(branch_half, "heads", axis=0, tiled=True)
    grad_out = dot_left(attended, grad_branch)
    grad_attended = dot_right(grad_branch, out_full).astype(jnp.bfloat16).reshape(tile_shape)
    probs_again = jnp.exp(masked_scores(query_tiles, key_tiles, allowed) - log_total)
    grad_probs = jnp.einsum(
        "bqhe,bkhe->bhqk", grad_attended, value_tiles, preferred_element_type=jnp.float32
    )
    inner = jnp.sum(probs_again * grad_probs, axis=-1, keepdims=True)
    grad_scores = (probs_again * (grad_probs - inner)).astype(jnp.bfloat16)
    grad_qs = jnp.einsum(
        "bhqk,bkhe->bqhe", grad_scores, key_tiles, preferred_element_type=jnp.float32
    )
    grad_key_proj = jnp.einsum(
        "bhqk,bqhe->bkhe", grad_scores, query_tiles, preferred_element_type=jnp.float32
    )
    grad_key_proj = grad_key_proj.reshape(tok_rows, local_hd).astype(jnp.bfloat16)
    grad_value_proj = jnp.einsum(
        "bhqk,bqhe->bkhe",
        probs_again.astype(jnp.bfloat16),
        grad_attended,
        preferred_element_type=jnp.float32,
    )
    grad_value_proj = grad_value_proj.reshape(tok_rows, local_hd).astype(jnp.bfloat16)
    grad_dim = (
        jnp.sum(grad_qs * query_proj.reshape(tile_shape), axis=(0, 1, 2))
        * scale_const
        * jax.nn.sigmoid(dim_scale)
    )
    grad_query_proj = (grad_qs * query_scale).reshape(tok_rows, local_hd).astype(jnp.bfloat16)
    grad_query = dot_left(normed_one, grad_query_proj)
    grad_key = dot_left(normed_one, grad_key_proj)
    grad_value = dot_left(normed_one, grad_value_proj)
    sum_query = jnp.sum(grad_query_proj.astype(jnp.float32), axis=0)
    sum_value = jnp.sum(grad_value_proj.astype(jnp.float32), axis=0)
    norm_terms = (
        dot_right(grad_query_proj, query_full)
        + dot_right(grad_key_proj, key_full)
        + dot_right(grad_value_proj, value_full)
    )
    grad_norm_one = lax.psum_scatter(
        norm_terms.astype(jnp.bfloat16), "heads", scatter_dimension=0, tiled=True
    ).astype(jnp.float32)
    back_one, grad_gain_one = norm_back(input_half, gain_attn, grad_norm_one)
    input_grad = grad_resid + back_one
    grad_up_w, grad_down_w = (
        lax.psum_scatter(grad_up, "wide", scatter_dimension=0, tiled=True),
        lax.psum_scatter(grad_down, "wide", scatter_dimension=1, tiled=True),
    )
    grad_query_w, grad_key_w, grad_value_w, grad_out_w = (
        lax.psum_scatter(grad_query, "wide", scatter_dimension=0, tiled=True),
        lax.psum_scatter(grad_key, "wide", scatter_dimension=0, tiled=True),
        lax.psum_scatter(grad_value, "wide", scatter_dimension=0, tiled=True),
        lax.psum_scatter(grad_out, "wide", scatter_dimension=1, tiled=True),
    )
    small_sums = lax.psum(
        (
            grad_gain_one,
            grad_gain_two,
            jnp.sum(grad_resid, axis=0),
            jnp.sum(grad_half, axis=0),
            grad_dim,
            place_part(sum_query, b_query.shape[0], head_index * local_hd),
            place_part(sum_value, b_value.shape[0], head_index * local_hd),
            bias_up_term,
        ),
        ("wide", "heads"),
    )
    (
        gain_one_sum,
        gain_two_sum,
        bias_out_sum,
        bias_down_sum,
        dim_sum,
        bias_query_sum,
        bias_value_sum,
        bias_up_sum,
    ) = small_sums
    return (
        output,
        input_grad,
        grad_query_w,
        grad_key_w,
        grad_value_w,
        grad_out_w,
        grad_up_w,
        grad_down_w,
        bias_query_sum,
        bias_value_sum,
        bias_out_sum,
        bias_up_sum,
        bias_down_sum,
        dim_sum,
        gain_one_sum,
        gain_two_sum,
    )


def solution(mesh):
    return jax.shard_map(
        shards,
        mesh=mesh,
        in_specs=(
            P("wide", None),
            P("wide"),
            P("wide", None),
            P("wide", "heads"),
            P("wide", "heads"),
            P("wide", "heads"),
            P("heads", "wide"),
            P("wide", "heads"),
            P("heads", "wide"),
            P(),
            P(),
            P(),
            P(),
            P(),
            P(),
            P(),
            P(),
        ),
        out_specs=(
            P(("wide", "heads"), None),
            P(("wide", "heads"), None),
            P("wide", "heads"),
            P("wide", "heads"),
            P("wide", "heads"),
            P("heads", "wide"),
            P("wide", "heads"),
            P("heads", "wide"),
            P(),
            P(),
            P(),
            P(),
            P(),
            P(),
            P(),
            P(),
        ),
        check_vma=False,
    )
```

profile of v0, /device:TPU:0, one launch (start us, length us, event | category | flops | bytes accessed | tf_op | source)
XLA Modules:
  0.0 1287.7 jit_solution(7532887947847363733)
XLA Ops:
  16.3 36.5 %all-gather.9.cloned.1.call-done = bf16[1280,640]{1,0:T(8,128)(2,1)} async-done(((bf16[80,640]{1,0:T(8,128)(2,1)}), bf16[1280,640]{1,0:T(8,128)(2,1)}) %all-gather.9.cloned.1.call-update) | async-done | bytes 1638416 | tf_op jit(solution)/shard_map/all_gather | solution.py:101
  60.2 33.6 %all-gather.11.cloned.1.call-done = bf16[1280,640]{1,0:T(8,128)(2,1)} async-done(((bf16[80,640]{1,0:T(8,128)(2,1)}), bf16[1280,640]{1,0:T(8,128)(2,1)}) %all-gather.11.cloned.1.call-update) | async-done | bytes 1638416 | tf_op jit(solution)/shard_map/all_gather | solution.py:99
  103.5 31.4 %all-gather.13.cloned.1.call-done = bf16[1280,640]{1,0:T(8,128)(2,1)} async-done(((bf16[80,640]{1,0:T(8,128)(2,1)}), bf16[1280,640]{1,0:T(8,128)(2,1)}) %all-gather.13.cloned.1.call-update) | async-done | bytes 1638416 | tf_op jit(solution)/shard_map/all_gather | solution.py:100
  197.0 10.0 fusion.42
  215.3 112.8 %reduce-scatter.11.cloned.1.call-done = f32[1024,1280]{1,0:T(8,128)} async-done(((f32[2048,1280]{1,0:T(8,128)}), f32[1024,1280]{1,0:T(8,128)}) %reduce-scatter.11.cloned.1.call-update) | async-done | bytes 5242896 | tf_op jit(solution)/shard_map/reduce_scatter | solution.py:129
  339.2 30.9 %all-gather.19.cloned.1.call-done = bf16[1280,640]{1,0:T(8,128)(2,1)} async-done(((bf16[80,640]{1,0:T(8,128)(2,1)}), bf16[1280,640]{1,0:T(8,128)(2,1)}) %all-gather.19.cloned.1.call-update) | async-done | bytes 1638416 | tf_op jit(solution)/shard_map/all_gather | solution.py:126
  370.1 69.6 %all-gather.17.cloned.1.call-done = bf16[2048,1280]{1,0:T(8,128)(2,1)} async-done(((bf16[1024,1280]{1,0:T(8,128)(2,1)}), bf16[2048,1280]{1,0:T(8,128)(2,1)}) %all-gather.17.cloned.1.call-update) | async-done | bytes 5242896 | tf_op jit(solution)/shard_map/all_gather | solution.py:134
  449.3 32.6 %all-gather.21.cloned.1.call-done = bf16[640,1280]{0,1:T(8,128)(2,1)} async-done(((bf16[640,80]{0,1:T(8,128)(2,1)}), bf16[640,1280]{0,1:T(8,128)(2,1)}) %all-gather.21.cloned.1.call-update) | async-done | bytes 1638416 | tf_op jit(solution)/shard_map/all_gather | solution.py:127
  481.9 10.0 convert_reduce_fusion.1
  500.8 10.5 convolution_convert_fusion.1
  511.4 52.7 %reduce-scatter.15.cloned.1.call-done = bf16[1024,1280]{1,0:T(8,128)(2,1)} async-done(((bf16[2048,1280]{1,0:T(8,128)(2,1)}), bf16[1024,1280]{1,0:T(8,128)(2,1)}) %reduce-scatter.15.cloned.1.call-update) | async-done | bytes 2621456 | tf_op jit(solution)/shard_map/reduce_scatter | solution.py:156
  569.2 63.0 %reduce-scatter.13.cloned.1.call-done = bf16[1024,1280]{1,0:T(8,128)(2,1)} async-done(((bf16[2048,1280]{1,0:T(8,128)(2,1)}), bf16[1024,1280]{1,0:T(8,128)(2,1)}) %reduce-scatter.13.cloned.1.call-update) | async-done | bytes 2621456 | tf_op jit(solution)/shard_map/reduce_scatter | solution.py:137
  643.7 68.2 %all-gather.23.cloned.1.call-done = bf16[2048,1280]{1,0:T(8,128)(2,1)} async-done(((bf16[1024,1280]{1,0:T(8,128)(2,1)}), bf16[2048,1280]{1,0:T(8,128)(2,1)}) %all-gather.23.cloned.1.call-update) | async-done | bytes 5242896 | tf_op jit(solution)/shard_map/all_gather | solution.py:171
  738.6 10.1 multiply_reduce_fusion.1
  780.0 11.3 add_convert_fusion
  801.3 10.3 fusion.60
  821.2 10.1 fusion.36
  862.3 41.1 %all-reduce = (f32[1280]{0:T(1024)}, f32[1280]{0:T(1024)}, f32[1280]{0:T(1024)}, f32[1280]{0:T(1024)}, f32[1280]{0:T(1024)}, /*index=5*/f32[80]{0:T(128)}, f32[1280]{0:T(1024)}, f32[1280]{0:T(1024)}) all-reduce(f32[1280]{0:T(1024)S(1)} %dynamic_update_slice.9, ...), channel_id=1, replica_groups=mesh['wide'=16,'heads'=2] {'wide','heads'}, use_global_device_ids=true, to_apply=%region_19.20 | all-reduce | flops 9040 | bytes 72320 | tf_op jit(solution)/shard_map/psum | solution.py:225
  909.9 19.7 %reduce-scatter.27.cloned.1.call-done = f32[80,640]{1,0:T(8,128)} async-done(((f32[1280,640]{1,0:T(8,128)}), f32[80,640]{1,0:T(8,128)}) %reduce-scatter.27.cloned.1.call-update) | async-done | bytes 204816 | tf_op jit(solution)/shard_map/reduce_scatter | solution.py:216
  929.6 70.0 %reduce-scatter.29.cloned.1.call-done = f32[640,80]{0,1:T(8,128)} async-done(((f32[640,1280]{0,1:T(8,128)}), f32[640,80]{0,1:T(8,128)}) %reduce-scatter.29.cloned.1.call-update) | async-done | bytes 204816 | tf_op jit(solution)/shard_map/reduce_scatter | solution.py:217
  999.6 70.5 %reduce-scatter.25.cloned.1.call-done = f32[640,80]{0,1:T(8,128)} async-done(((f32[640,1280]{0,1:T(8,128)}), f32[640,80]{0,1:T(8,128)}) %reduce-scatter.25.cloned.1.call-update) | async-done | bytes 204816 | tf_op jit(solution)/shard_map/reduce_scatter | solution.py:223
  1070.1 70.0 %reduce-scatter.19.cloned.1.call-done = f32[80,640]{1,0:T(8,128)} async-done(((f32[1280,640]{1,0:T(8,128)}), f32[80,640]{1,0:T(8,128)}) %reduce-scatter.19.cloned.1.call-update) | async-done | bytes 204816 | tf_op jit(solution)/shard_map/reduce_scatter | solution.py:220
  1140.2 70.4 %reduce-scatter.21.cloned.1.call-done = f32[80,640]{1,0:T(8,128)} async-done(((f32[1280,640]{1,0:T(8,128)}), f32[80,640]{1,0:T(8,128)}) %reduce-scatter.21.cloned.1.call-update) | async-done | bytes 204816 | tf_op jit(solution)/shard_map/reduce_scatter | solution.py:221
  1210.6 70.0 %reduce-scatter.23.cloned.1.call-done = f32[80,640]{1,0:T(8,128)} async-done(((f32[1280,640]{1,0:T(8,128)}), f32[80,640]{1,0:T(8,128)}) %reduce-scatter.23.cloned.1.call-update) | async-done | bytes 204816 | tf_op jit(solution)/shard_map/reduce_scatter | solution.py:222
  (170 shorter events, 257.1 us)
Async XLA Ops:
  7.2 45.7 %all-gather.9.cloned.1.call-start = ((), (), s32[]{:S(2)}) async-start(), calls=%async_computation.10 | async-start | bytes 1740800 | tf_op jit(solution)/shard_map/all_gather | solution.py:101
  7.9 85.9 %all-gather.11.cloned.1.call-start = ((), (), s32[]{:S(2)}) async-start(), calls=%async_computation.11 | async-start | bytes 1740800 | tf_op jit(solution)/shard_map/all_gather | solution.py:99
  8.7 126.2 %all-gather.13.cloned.1.call-start = ((), (), s32[]{:S(2)}) async-start(), calls=%async_computation.12 | async-start | bytes 1740800 | tf_op jit(solution)/shard_map/all_gather | solution.py:100
  9.4 187.6 %all-gather.15.cloned.1.call-start = ((), (), s32[]{:S(2)}) async-start(), calls=%async_computation.13 | async-start | bytes 1740800 | tf_op jit(solution)/shard_map/all_gather | solution.py:102
  10.0 318.2 %reduce-scatter.11.cloned.1.call-start = ((), (), s32[]{:S(2)}) async-start(), calls=%async_computation.14 | async-start | bytes 15728640 | tf_op jit(solution)/shard_map/reduce_scatter | solution.py:129
  15.9 119.0 %copy-start.21 = (f32[2048]{0:T(1024)}, f32[2048]{0:T(1024)S(1)}, u32[]{:S(2)}) copy-start(f32[2048]{0:T(1024)S(1)} %add_rsqrt_fusion) | copy-start | bytes 24580
  207.0 163.1 %all-gather.19.cloned.1.call-start = ((), (), s32[]{:S(2)}) async-start(), calls=%async_computation.16 | async-start | bytes 1740800 | tf_op jit(solution)/shard_map/all_gather | solution.py:126
  207.6 120.5 %copy-start.19 = (f32[1280]{0:T(1024)S(1)}, f32[1280]{0:T(1024)}, u32[]{:S(2)}) copy-start(f32[1280]{0:T(1024)} %param.28) | copy-start | bytes 15364
  207.6 232.1 %all-gather.17.cloned.1.call-start = ((), (), s32[]{:S(2)}) async-start(), calls=%async_computation.15 | async-start | bytes 7864320 | tf_op jit(solution)/shard_map/all_gather | solution.py:134
  215.3 121.0 %copy-start.14 = (f32[1280]{0:T(1024)S(1)}, f32[1280]{0:T(1024)}, u32[]{:S(2)}) copy-start(f32[1280]{0:T(1024)} %param.33) | copy-start | bytes 15364
  338.3 143.6 %all-gather.21.cloned.1.call-start = ((), (), s32[]{:S(2)}) async-start(), calls=%async_computation.17 | async-start | bytes 1740800 | tf_op jit(solution)/shard_map/all_gather | solution.py:127
  339.1 225.1 %reduce-scatter.15.cloned.1.call-start = ((), (), s32[]{:S(2)}) async-start(), calls=%async_computation.19 | async-start | bytes 7864320 | tf_op jit(solution)/shard_map/reduce_scatter | solution.py:156
  499.4 132.7 %reduce-scatter.13.cloned.1.call-start = ((), (), s32[]{:S(2)}) async-start(), calls=%async_computation.18 | async-start | bytes 7864320 | tf_op jit(solution)/shard_map/reduce_scatter | solution.py:137
  511.4 120.8 %copy-start.20 = (f32[1280]{0:T(1024)S(1)}, f32[1280]{0:T(1024)}, u32[]{:S(2)}) copy-start(f32[1280]{0:T(1024)} %param.30) | copy-start | bytes 15364
  511.4 200.5 %all-gather.23.cloned.1.call-start = ((), (), s32[]{:S(2)}) async-start(), calls=%async_computation.20 | async-start | bytes 7864320 | tf_op jit(solution)/shard_map/all_gather | solution.py:171
  564.1 68.0 %copy-start.8 = (bf16[1024,1280]{1,0:T(8,128)(2,1)S(1)}, bf16[1024,1280]{1,0:T(8,128)(2,1)}, u32[]{:S(2)}) copy-start(bf16[1024,1280]{1,0:T(8,128)(2,1)} %reduce-scatter.15.cloned.1.call-done) | copy-start | bytes 7864324
  643.2 214.0 %reduce-scatter.17.cloned.1.call-start = ((), (), s32[]{:S(2)}) async-start(), calls=%async_computation.21 | async-start | bytes 7864320 | tf_op jit(solution)/shard_map/reduce_scatter | solution.py:210
  791.4 138.2 %reduce-scatter.27.cloned.1.call-start = ((), (), s32[]{:S(2)}) async-start(), calls=%async_computation.26 | async-start | bytes 3481600 | tf_op jit(solution)/shard_map/reduce_scatter | solution.py:216
  800.9 198.7 %reduce-scatter.29.cloned.1.call-start = ((), (), s32[]{:S(2)}) async-start(), calls=%async_computation.27 | async-start | bytes 3481600 | tf_op jit(solution)/shard_map/reduce_scatter | solution.py:217
  811.7 258.5 %reduce-scatter.25.cloned.1.call-start = ((), (), s32[]{:S(2)}) async-start(), calls=%async_computation.25 | async-start | bytes 3481600 | tf_op jit(solution)/shard_map/reduce_scatter | solution.py:223
  821.0 319.2 %reduce-scatter.19.cloned.1.call-start = ((), (), s32[]{:S(2)}) async-start(), calls=%async_computation.22 | async-start | bytes 3481600 | tf_op jit(solution)/shard_map/reduce_scatter | solution.py:220
  831.4 379.3 %reduce-scatter.21.cloned.1.call-start = ((), (), s32[]{:S(2)}) async-start(), calls=%async_computation.23 | async-start | bytes 3481600 | tf_op jit(solution)/shard_map/reduce_scatter | solution.py:221
  841.2 439.4 %reduce-scatter.23.cloned.1.call-start = ((), (), s32[]{:S(2)}) async-start(), calls=%async_computation.24 | async-start | bytes 3481600 | tf_op jit(solution)/shard_map/reduce_scatter | solution.py:222
  857.2 46.1 %copy-start.5 = (bf16[1024,1280]{1,0:T(8,128)(2,1)S(1)}, bf16[1024,1280]{1,0:T(8,128)(2,1)}, u32[]{:S(2)}) copy-start(bf16[1024,1280]{1,0:T(8,128)(2,1)} %reduce-scatter.17.cloned.1.call-done) | copy-start | bytes 7864324
  (28 other events, 304.3 us)
Sparse Core Ops, SparseCore 0:
  10.2 42.6 all-gather.8
  55.0 38.8 all-gather.10
  96.1 38.8 all-gather.12
  136.9 38.8 all-gather.14
  207.2 120.9 reduce-scatter.10
  330.2 39.9 all-gather.18
  372.3 67.4 all-gather.16
  441.9 39.9 all-gather.20
  499.5 64.5 reduce-scatter.14
  566.4 65.6 reduce-scatter.12
  643.3 68.5 all-gather.22
  791.5 65.6 reduce-scatter.16
  862.1 67.4 reduce-scatter.26
  933.9 65.7 reduce-scatter.28
  1004.4 65.7 reduce-scatter.24
  1074.4 65.7 reduce-scatter.18
  1144.9 65.6 reduce-scatter.20
  1214.9 65.7 reduce-scatter.22
where the time goes:
time: 1300 us; the launch traced here: 1290 us
  waiting for transfers between devices  912 us (70%)
  matrix products  195 us (15%)
  local copies, waits for them, and re-layouts  70.2 us (5%)
  other arithmetic  53.1 us (4%)
  blocking collectives  41.1 us (3%)
  between operations  15 us (1%)
    reduce_scatter x1, waiting for transfers between devices, shards(): lax.psum_scatter(dot_plain(attended, out_full), 'heads', scatter_dimensio...  113 us
    reduce_scatter x1, waiting for transfers between devices, shards(): lax.psum_scatter(grad_out, 'wide', scatter_dimension=1, tiled=True)  70.5 us
    reduce_scatter x1, waiting for transfers between devices, shards(): lax.psum_scatter(grad_key, 'wide', scatter_dimension=0, tiled=True)  70.4 us
    reduce_scatter x1, waiting for transfers between devices, shards(): lax.psum_scatter(grad_value, 'wide', scatter_dimension=0, tiled=True)  70 us
    reduce_scatter x1, waiting for transfers between devices, shards(): lax.psum_scatter(grad_query, 'wide', scatter_dimension=0, tiled=True)  70 us
    reduce_scatter x1, waiting for transfers between devices, shards(): lax.psum_scatter(grad_down, 'wide', scatter_dimension=1, tiled=True)  70 us
    all_gather x1, waiting for transfers between devices, shards(): normed_two = lax.all_gather(normed_half, 'heads', axis=0, tiled=True)  69.6 us
    all_gather x1, waiting for transfers between devices, shards(): grad_branch = lax.all_gather(branch_half, 'heads', axis=0, tiled=True)  68.2 us
  transfers between devices with their start and end apart: 18, of which 17 were waited for; matrix products, arithmetic and copies ran while one was open for 15% of the time, Pallas kernels for 0%

commit v1 on v0

--- a/solution.py
+++ b/solution.py
@@ -222,19 +222,17 @@
         lax.psum_scatter(grad_value, "wide", scatter_dimension=0, tiled=True),
         lax.psum_scatter(grad_out, "wide", scatter_dimension=1, tiled=True),
     )
-    small_sums = lax.psum(
-        (
-            grad_gain_one,
-            grad_gain_two,
-            jnp.sum(grad_resid, axis=0),
-            jnp.sum(grad_half, axis=0),
-            grad_dim,
-            place_part(sum_query, b_query.shape[0], head_index * local_hd),
-            place_part(sum_value, b_value.shape[0], head_index * local_hd),
-            bias_up_term,
-        ),
-        ("wide", "heads"),
-    )
+    incoming_x = (
+        grad_gain_one,
+        grad_gain_two,
+        jnp.sum(grad_resid, axis=0),
+        jnp.sum(grad_half, axis=0),
+        grad_dim,
+        place_part(sum_query, b_query.shape[0], head_index * local_hd),
+        place_part(sum_value, b_value.shape[0], head_index * local_hd),
+        bias_up_term,
+    )
+    small_sums = lax.psum(lax.psum(incoming_x, axis_name="heads"), axis_name="wide")
     (
         gain_one_sum,
         gain_two_sum,

time: 1300 us -> 1300 us (level)
  waiting for transfers between devices: 912 us -> 884 us
  blocking collectives: 41.1 us -> 68.6 us
    psum x1 -> x2, blocking collectives: 41.1 us -> 68.6 us  [the longest x1 60.9 us: shards(): lax.psum(lax.psum(incoming_x, axis_name='heads'), axis_name='wide')]
    reduce_scatter x1, waiting for transfers between devices: 19.7 us -> 0.01 us  [shards(): lax.psum_scatter(grad_up, 'wide', scatter_dimension=0, tiled=True)]
  transfers between devices with their start and end apart: 18 -> 18, of which waited for: 17 -> 16; matrix products, arithmetic and copies ran while one was open for 15% -> 15% of each run, Pallas kernels for 0% -> 0%
where the time goes in v1:
time: 1300 us; the launch traced here: 1290 us
  waiting for transfers between devices  884 us (68%)
  matrix products  195 us (15%)
  local copies, waits for them, and re-layouts  70.2 us (5%)
  blocking collectives  68.6 us (5%)
  other arithmetic  53 us (4%)
  between operations  15 us (1%)
    reduce_scatter x1, waiting for transfers between devices, shards(): lax.psum_scatter(dot_plain(attended, out_full), 'heads', scatter_dimensio...  113 us
    reduce_scatter x1, waiting for transfers between devices, shards(): lax.psum_scatter(grad_key, 'wide', scatter_dimension=0, tiled=True)  70.5 us
    reduce_scatter x1, waiting for transfers between devices, shards(): lax.psum_scatter(grad_out, 'wide', scatter_dimension=1, tiled=True)  70.5 us
    reduce_scatter x1, waiting for transfers between devices, shards(): lax.psum_scatter(grad_value, 'wide', scatter_dimension=0, tiled=True)  70.1 us
    reduce_scatter x1, waiting for transfers between devices, shards(): lax.psum_scatter(grad_query, 'wide', scatter_dimension=0, tiled=True)  70.1 us
    all_gather x1, waiting for transfers between devices, shards(): normed_two = lax.all_gather(normed_half, 'heads', axis=0, tiled=True)  69.6 us
    all_gather x1, waiting for transfers between devices, shards(): grad_branch = lax.all_gather(branch_half, 'heads', axis=0, tiled=True)  68.2 us
    reduce_scatter x1, waiting for transfers between devices, shards(): lax.psum_scatter(dot_plain(activated, down_full).astype(jnp.bfloat16), 'h...  63 us
  transfers between devices with their start and end apart: 18, of which 16 were waited for; matrix products, arithmetic and copies ran while one was open for 15% of the time, Pallas kernels for 0%

profile of v1, /device:TPU:0, one launch (start us, length us, event | category | flops | bytes accessed | tf_op | source)
XLA Modules:
  0.0 1287.5 jit_solution(2870112703341335290)
XLA Ops:
  16.3 36.5 %all-gather.9.cloned.1.call-done = bf16[1280,640]{1,0:T(8,128)(2,1)} async-done(((bf16[80,640]{1,0:T(8,128)(2,1)}), bf16[1280,640]{1,0:T(8,128)(2,1)}) %all-gather.9.cloned.1.call-update) | async-done | bytes 1638416 | tf_op jit(solution)/shard_map/all_gather | solution.py:101
  60.2 33.6 %all-gather.11.cloned.1.call-done = bf16[1280,640]{1,0:T(8,128)(2,1)} async-done(((bf16[80,640]{1,0:T(8,128)(2,1)}), bf16[1280,640]{1,0:T(8,128)(2,1)}) %all-gather.11.cloned.1.call-update) | async-done | bytes 1638416 | tf_op jit(solution)/shard_map/all_gather | solution.py:99
  103.5 31.4 %all-gather.13.cloned.1.call-done = bf16[1280,640]{1,0:T(8,128)(2,1)} async-done(((bf16[80,640]{1,0:T(8,128)(2,1)}), bf16[1280,640]{1,0:T(8,128)(2,1)}) %all-gather.13.cloned.1.call-update) | async-done | bytes 1638416 | tf_op jit(solution)/shard_map/all_gather | solution.py:100
  197.0 10.0 fusion.42
  215.4 112.8 %reduce-scatter.11.cloned.1.call-done = f32[1024,1280]{1,0:T(8,128)} async-done(((f32[2048,1280]{1,0:T(8,128)}), f32[1024,1280]{1,0:T(8,128)}) %reduce-scatter.11.cloned.1.call-update) | async-done | bytes 5242896 | tf_op jit(solution)/shard_map/reduce_scatter | solution.py:129
  339.2 30.9 %all-gather.19.cloned.1.call-done = bf16[1280,640]{1,0:T(8,128)(2,1)} async-done(((bf16[80,640]{1,0:T(8,128)(2,1)}), bf16[1280,640]{1,0:T(8,128)(2,1)}) %all-gather.19.cloned.1.call-update) | async-done | bytes 1638416 | tf_op jit(solution)/shard_map/all_gather | solution.py:126
  370.1 69.6 %all-gather.17.cloned.1.call-done = bf16[2048,1280]{1,0:T(8,128)(2,1)} async-done(((bf16[1024,1280]{1,0:T(8,128)(2,1)}), bf16[2048,1280]{1,0:T(8,128)(2,1)}) %all-gather.17.cloned.1.call-update) | async-done | bytes 5242896 | tf_op jit(solution)/shard_map/all_gather | solution.py:134
  449.3 32.6 %all-gather.21.cloned.1.call-done = bf16[640,1280]{0,1:T(8,128)(2,1)} async-done(((bf16[640,80]{0,1:T(8,128)(2,1)}), bf16[640,1280]{0,1:T(8,128)(2,1)}) %all-gather.21.cloned.1.call-update) | async-done | bytes 1638416 | tf_op jit(solution)/shard_map/all_gather | solution.py:127
  481.9 10.0 convert_reduce_fusion.1
  500.8 10.5 convolution_convert_fusion.1
  511.3 52.8 %reduce-scatter.15.cloned.1.call-done = bf16[1024,1280]{1,0:T(8,128)(2,1)} async-done(((bf16[2048,1280]{1,0:T(8,128)(2,1)}), bf16[1024,1280]{1,0:T(8,128)(2,1)}) %reduce-scatter.15.cloned.1.call-update) | async-done | bytes 2621456 | tf_op jit(solution)/shard_map/reduce_scatter | solution.py:156
  569.2 63.0 %reduce-scatter.13.cloned.1.call-done = bf16[1024,1280]{1,0:T(8,128)(2,1)} async-done(((bf16[2048,1280]{1,0:T(8,128)(2,1)}), bf16[1024,1280]{1,0:T(8,128)(2,1)}) %reduce-scatter.13.cloned.1.call-update) | async-done | bytes 2621456 | tf_op jit(solution)/shard_map/reduce_scatter | solution.py:137
  643.7 68.2 %all-gather.23.cloned.1.call-done = bf16[2048,1280]{1,0:T(8,128)(2,1)} async-done(((bf16[1024,1280]{1,0:T(8,128)(2,1)}), bf16[2048,1280]{1,0:T(8,128)(2,1)}) %all-gather.23.cloned.1.call-update) | async-done | bytes 5242896 | tf_op jit(solution)/shard_map/all_gather | solution.py:171
  738.5 10.1 multiply_reduce_fusion.1
  780.0 11.3 add_convert_fusion
  801.3 10.3 fusion.60
  821.2 10.1 fusion.36
  831.4 9.8 fusion.32
  869.9 60.9 %all-reduce = (f32[1280]{0:T(1024)}, f32[1280]{0:T(1024)}, f32[1280]{0:T(1024)}, f32[1280]{0:T(1024)}, f32[1280]{0:T(1024)}, /*index=5*/f32[80]{0:T(128)}, f32[1280]{0:T(1024)}, f32[1280]{0:T(1024)}) all-reduce(f32[1280]{0:T(1024)S(1)} %get-tuple-element.28, ...), channel_id=1, replica_groups=mesh['wide'=16,'heads'=2] {'wide'}, use_global_device_ids=true, to_apply=%region_20.21 | all-reduce | flops 9040 | bytes 72320 | tf_op jit(solution)/shard_map/psum | solution.py:235
  937.3 62.0 %reduce-scatter.29.cloned.1.call-done = f32[640,80]{0,1:T(8,128)} async-done(((f32[640,1280]{0,1:T(8,128)}), f32[640,80]{0,1:T(8,128)}) %reduce-scatter.29.cloned.1.call-update) | async-done | bytes 204816 | tf_op jit(solution)/shard_map/reduce_scatter | solution.py:217
  999.2 70.5 %reduce-scatter.25.cloned.1.call-done = f32[640,80]{0,1:T(8,128)} async-done(((f32[640,1280]{0,1:T(8,128)}), f32[640,80]{0,1:T(8,128)}) %reduce-scatter.25.cloned.1.call-update) | async-done | bytes 204816 | tf_op jit(solution)/shard_map/reduce_scatter | solution.py:223
  1069.7 70.1 %reduce-scatter.19.cloned.1.call-done = f32[80,640]{1,0:T(8,128)} async-done(((f32[1280,640]{1,0:T(8,128)}), f32[80,640]{1,0:T(8,128)}) %reduce-scatter.19.cloned.1.call-update) | async-done | bytes 204816 | tf_op jit(solution)/shard_map/reduce_scatter | solution.py:220
  1139.8 70.5 %reduce-scatter.21.cloned.1.call-done = f32[80,640]{1,0:T(8,128)} async-done(((f32[1280,640]{1,0:T(8,128)}), f32[80,640]{1,0:T(8,128)}) %reduce-scatter.21.cloned.1.call-update) | async-done | bytes 204816 | tf_op jit(solution)/shard_map/reduce_scatter | solution.py:221
  1210.4 70.1 %reduce-scatter.23.cloned.1.call-done = f32[80,640]{1,0:T(8,128)} async-done(((f32[1280,640]{1,0:T(8,128)}), f32[80,640]{1,0:T(8,128)}) %reduce-scatter.23.cloned.1.call-update) | async-done | bytes 204816 | tf_op jit(solution)/shard_map/reduce_scatter | solution.py:222
  (171 shorter events, 254.9 us)
Async XLA Ops:
  7.2 45.7 %all-gather.9.cloned.1.call-start = ((), (), s32[]{:S(2)}) async-start(), calls=%async_computation.10 | async-start | bytes 1740800 | tf_op jit(solution)/shard_map/all_gather | solution.py:101
  7.9 85.9 %all-gather.11.cloned.1.call-start = ((), (), s32[]{:S(2)}) async-start(), calls=%async_computation.11 | async-start | bytes 1740800 | tf_op jit(solution)/shard_map/all_gather | solution.py:99
  8.7 126.2 %all-gather.13.cloned.1.call-start = ((), (), s32[]{:S(2)}) async-start(), calls=%async_computation.12 | async-start | bytes 1740800 | tf_op jit(solution)/shard_map/all_gather | solution.py:100
  9.4 187.6 %all-gather.15.cloned.1.call-start = ((), (), s32[]{:S(2)}) async-start(), calls=%async_computation.13 | async-start | bytes 1740800 | tf_op jit(solution)/shard_map/all_gather | solution.py:102
  10.0 318.2 %reduce-scatter.11.cloned.1.call-start = ((), (), s32[]{:S(2)}) async-start(), calls=%async_computation.14 | async-start | bytes 15728640 | tf_op jit(solution)/shard_map/reduce_scatter | solution.py:129
  15.9 119.0 %copy-start.21 = (f32[2048]{0:T(1024)}, f32[2048]{0:T(1024)S(1)}, u32[]{:S(2)}) copy-start(f32[2048]{0:T(1024)S(1)} %add_rsqrt_fusion) | copy-start | bytes 24580
  207.1 163.1 %all-gather.19.cloned.1.call-start = ((), (), s32[]{:S(2)}) async-start(), calls=%async_computation.16 | async-start | bytes 1740800 | tf_op jit(solution)/shard_map/all_gather | solution.py:126
  207.7 120.5 %copy-start.19 = (f32[1280]{0:T(1024)S(1)}, f32[1280]{0:T(1024)}, u32[]{:S(2)}) copy-start(f32[1280]{0:T(1024)} %param.28) | copy-start | bytes 15364
  207.7 232.1 %all-gather.17.cloned.1.call-start = ((), (), s32[]{:S(2)}) async-start(), calls=%async_computation.15 | async-start | bytes 7864320 | tf_op jit(solution)/shard_map/all_gather | solution.py:134
  215.4 121.0 %copy-start.14 = (f32[1280]{0:T(1024)S(1)}, f32[1280]{0:T(1024)}, u32[]{:S(2)}) copy-start(f32[1280]{0:T(1024)} %param.33) | copy-start | bytes 15364
  338.3 143.5 %all-gather.21.cloned.1.call-start = ((), (), s32[]{:S(2)}) async-start(), calls=%async_computation.17 | async-start | bytes 1740800 | tf_op jit(solution)/shard_map/all_gather | solution.py:127
  339.1 225.0 %reduce-scatter.15.cloned.1.call-start = ((), (), s32[]{:S(2)}) async-start(), calls=%async_computation.19 | async-start | bytes 7864320 | tf_op jit(solution)/shard_map/reduce_scatter | solution.py:156
  499.4 132.7 %reduce-scatter.13.cloned.1.call-start = ((), (), s32[]{:S(2)}) async-start(), calls=%async_computation.18 | async-start | bytes 7864320 | tf_op jit(solution)/shard_map/reduce_scatter | solution.py:137
  511.3 120.8 %copy-start.20 = (f32[1280]{0:T(1024)S(1)}, f32[1280]{0:T(1024)}, u32[]{:S(2)}) copy-start(f32[1280]{0:T(1024)} %param.30) | copy-start | bytes 15364
  511.3 200.6 %all-gather.23.cloned.1.call-start = ((), (), s32[]{:S(2)}) async-start(), calls=%async_computation.20 | async-start | bytes 7864320 | tf_op jit(solution)/shard_map/all_gather | solution.py:171
  564.1 68.0 %copy-start.8 = (bf16[1024,1280]{1,0:T(8,128)(2,1)S(1)}, bf16[1024,1280]{1,0:T(8,128)(2,1)}, u32[]{:S(2)}) copy-start(bf16[1024,1280]{1,0:T(8,128)(2,1)} %reduce-scatter.15.cloned.1.call-done) | copy-start | bytes 7864324
  643.2 214.0 %reduce-scatter.17.cloned.1.call-start = ((), (), s32[]{:S(2)}) async-start(), calls=%async_computation.21 | async-start | bytes 7864320 | tf_op jit(solution)/shard_map/reduce_scatter | solution.py:210
  791.4 145.9 %reduce-scatter.27.cloned.1.call-start = ((), (), s32[]{:S(2)}) async-start(), calls=%async_computation.26 | async-start | bytes 3481600 | tf_op jit(solution)/shard_map/reduce_scatter | solution.py:216
  800.9 198.3 %reduce-scatter.29.cloned.1.call-start = ((), (), s32[]{:S(2)}) async-start(), calls=%async_computation.27 | async-start | bytes 3481600 | tf_op jit(solution)/shard_map/reduce_scatter | solution.py:217
  811.7 258.1 %reduce-scatter.25.cloned.1.call-start = ((), (), s32[]{:S(2)}) async-start(), calls=%async_computation.25 | async-start | bytes 3481600 | tf_op jit(solution)/shard_map/reduce_scatter | solution.py:223
  821.0 318.8 %reduce-scatter.19.cloned.1.call-start = ((), (), s32[]{:S(2)}) async-start(), calls=%async_computation.22 | async-start | bytes 3481600 | tf_op jit(solution)/shard_map/reduce_scatter | solution.py:220
  831.4 379.0 %reduce-scatter.21.cloned.1.call-start = ((), (), s32[]{:S(2)}) async-start(), calls=%async_computation.23 | async-start | bytes 3481600 | tf_op jit(solution)/shard_map/reduce_scatter | solution.py:221
  841.2 439.2 %reduce-scatter.23.cloned.1.call-start = ((), (), s32[]{:S(2)}) async-start(), calls=%async_computation.24 | async-start | bytes 3481600 | tf_op jit(solution)/shard_map/reduce_scatter | solution.py:222
  857.2 73.6 %copy-start.5 = (bf16[1024,1280]{1,0:T(8,128)(2,1)S(1)}, bf16[1024,1280]{1,0:T(8,128)(2,1)}, u32[]{:S(2)}) copy-start(bf16[1024,1280]{1,0:T(8,128)(2,1)} %reduce-scatter.17.cloned.1.call-done) | copy-start | bytes 7864324
  (28 other events, 304.4 us)
Sparse Core Ops, SparseCore 0:
  10.2 42.6 all-gather.8
  55.0 38.8 all-gather.10
  96.1 38.8 all-gather.12
  136.9 38.8 all-gather.14
  207.2 120.9 reduce-scatter.10
  330.2 39.8 all-gather.18
  372.2 67.4 all-gather.16
  441.9 39.9 all-gather.20
  499.5 64.5 reduce-scatter.14
  566.4 65.6 reduce-scatter.12
  643.3 68.5 all-gather.22
  791.5 65.6 reduce-scatter.16
  862.1 67.1 reduce-scatter.26
  933.5 65.6 reduce-scatter.28
  1004.0 65.7 reduce-scatter.24
  1074.0 65.7 reduce-scatter.18
  1144.5 65.7 reduce-scatter.20
  1214.6 65.7 reduce-scatter.22
